TPU v7x, 512 devices: a whole 4x8x8 slice. The times are simulated.
512 devices in a mesh: seq: 64 (over z, y), kvh: 8 (over x, core).
Axes of the slice: x: 4, y: 8, z: 8, core: 2. Of those that a mesh axis runs over, the one named last changes fastest.
Arguments:
- queries: bfloat16 [128, 8192], P(None, 'kvh'), may hold values from -256 to 256
- new_keys: bfloat16 [128, 1024], P(None, 'kvh'), may hold values from -40 to 40
- new_values: bfloat16 [128, 1024], P(None, 'kvh'), may hold values from -6 to 6
- prefix_keys: bfloat16 [131072, 1024], P('seq', 'kvh'), may hold values from -8 to 8
- prefix_values: bfloat16 [131072, 1024], P('seq', 'kvh'), may hold values from -6 to 6
- suffix_keys: bfloat16 [128, 1024, 1024], P(None, 'seq', 'kvh'), may hold values from -16 to 16
- suffix_values: bfloat16 [128, 1024, 1024], P(None, 'seq', 'kvh'), may hold values from -6 to 6
- prefix_offsets: int32 [128], replicated, may hold values from 2 to 131072, as said below
- suffix_lengths: int32 [128], replicated, may hold values from 0 to 1024, as said below
- out_weight: bfloat16 [8192, 8192], P('kvh', 'seq'), may hold values from -0.0625 to 0.0625
- residual: bfloat16 [128, 8192], P(None, 'seq'), may hold values from -70 to 70
- norm_gain: float32 [8192], P('seq'), may hold values from 0.1 to 1.9
- w_gate: bfloat16 [8192, 28672], P('seq', 'kvh'), may hold values from -0.0625 to 0.0625
- w_up: bfloat16 [8192, 28672], P('seq', 'kvh'), may hold values from -0.0625 to 0.0625
- w_down: bfloat16 [28672, 8192], P('kvh', 'seq'), may hold values from -0.03125 to 0.03125
Outputs:
- attention: bfloat16 [128, 8192], P(None, 'kvh')
- mixed: bfloat16 [128, 8192], P(None, 'seq')
Inputs may be any that keep to these rules, and one draw needn't show every extreme that they name: Branch b sees the prefix positions below prefix_offsets[b]; some branch sees all 131072. Branch b's suffix positions below suffix_lengths[b] are live; some branch has all 1024.
All inputs are finite; a program needn't handle non-finite values.
Results may differ from a plain program's by a relative error of at most 0.007.
Values may be sent and summed in bfloat16 or wider, within the bound.
No kernel may reach another device: no remote copies, remote signals or barrier semaphores. Data moves between devices by JAX's collectives and lax.ppermute only.
A program may use at most 192 MiB of HBM per device.

v0:
```python
import functools
import math

import jax
import jax.numpy as jnp
from jax import lax
from jax.experimental import pallas as pl
from jax.experimental.pallas import tpu as pltpu
from jax.sharding import PartitionSpec as P

HD = 128
D = 8192
SIDE = 8
Z_GROUPS = [[z * SIDE + y for z in range(SIDE)] for y in range(SIDE)]
Y_GROUPS = [[z * SIDE + y for y in range(SIDE)] for z in range(SIDE)]
QUAD = 4
BLOCKS = SIDE * SIDE // QUAD


def seq_at(p, q):
    return (q // (SIDE // 2) * 2 + p // 2) * SIDE + q % (SIDE // 2) * 2 + p % 2


P_GROUPS = [[seq_at(p, q) for p in range(QUAD)] for q in range(BLOCKS)]
Q_GROUPS = [[seq_at(p, q) for q in range(BLOCKS)] for p in range(QUAD)]
SEQ_ORDER = [seq_at(p, q) for p in range(QUAD) for q in range(BLOCKS)]
NEG_FILL = -1e30
EPSILON = 1e-05
SCALE_LOG2 = math.log2(math.e) / math.sqrt(HD)
EXTRA = 16
PIECES = 4
MIB = 2**20


def dot_nt(a, b):
    return lax.dot_general(a, b, (((1,), (1,)), ((), ())), preferred_element_type=jnp.float32)


def parts_of(x, count):
    parts = []
    for _ in range(count):
        part = x.astype(jnp.bfloat16).astype(jnp.float32)
        parts.append(part)
        x = x - part
    return parts


def padded(rows, count):
    return jnp.concatenate(rows + [jnp.zeros_like(rows[0])] * (count - len(rows)), axis=0)


def with_ones(values):
    return jnp.concatenate([values.T, jnp.ones((EXTRA, values.shape[0]), values.dtype)], axis=0)


def bring(sources, targets, sems):
    waits = []
    for i, (source, target) in enumerate(zip(sources, targets)):
        size = source.shape[0] // PIECES
        copies = []
        for j in range(PIECES):
            part = pl.ds(j * size, size)
            copy = pltpu.make_async_copy(source.at[part], target.at[part], sems.at[i, j])
            copy.start()
            copies.append(copy)
        waits.append(lambda copies=copies: [copy.wait() for copy in copies])
    return waits


def own_place():
    seq = lax.axis_index("seq")
    return seq // SIDE % 2 * 2 + seq % 2


def head_rows(block, heads):
    return jnp.concatenate([block[:, h * HD : (h + 1) * HD] for h in range(heads)], axis=0)


def over(x, power):
    assert power & (power - 1) == 0
    return lax.shift_right_logical(x, power.bit_length() - 1)


def by_column(bands, band, numbers, shifts):
    size = numbers.shape[1]
    lane = lax.broadcasted_iota(jnp.int32, (bands, size), 1)
    mine = over(lane, band) == lax.broadcasted_iota(jnp.int32, (bands, size), 0)
    digits = []
    for i, shift in enumerate(shifts):
        digit = lax.shift_right_logical(numbers, shift)
        if i > 0:
            digit = digit & 31
        digits.append(jnp.where(mine, digit.astype(jnp.float32), 0.0))
    row = lax.broadcasted_iota(jnp.int32, (size, size), 0)
    col = lax.broadcasted_iota(jnp.int32, (size, size), 1)
    spread = jnp.where(row & (band - 1) == col & (band - 1), 1.0, 0.0).astype(jnp.bfloat16)
    got = jnp.dot(
        jnp.concatenate(digits, axis=0).astype(jnp.bfloat16), spread,
        preferred_element_type=jnp.float32,
    ).astype(jnp.int32)
    return sum(got[i * bands : (i + 1) * bands] << shift for i, shift in enumerate(shifts))


def attend(bands, band, heads, offsets_ref, lengths_ref, q_hbm, k_hbm, v_hbm, sk_hbm, sv_hbm, out_ref,
           q_ref, k_ref, v_ref, sk_ref, sv_ref, vt_ref, off_ref, len_ref, tail_pos_ref,
           sems):
    context = k_ref.shape[0]
    tail = sk_ref.shape[1]
    cols = heads * band
    seq = lax.axis_index("seq")
    waits = bring(
        (q_hbm, k_hbm, sk_hbm, v_hbm, sv_hbm), (q_ref, k_ref, sk_ref, v_ref, sv_ref), sems
    )
    off_ref[...] = by_column(bands, band, offsets_ref[...], (10, 5, 0))
    len_ref[...] = by_column(bands, band, lengths_ref[...], (5, 0))
    row = lax.broadcasted_iota(jnp.int32, tail_pos_ref.shape, 0)
    col = lax.broadcasted_iota(jnp.int32, tail_pos_ref.shape, 1)
    own_branch = over(row, tail) == col & (band - 1)
    tail_pos_ref[...] = jnp.where(own_branch, row & (tail - 1), 2**20)

    def queries_of(g):
        return head_rows(q_ref[pl.ds(pl.multiple_of(g * band, band), band), :], heads)

    def pair(p, first):
        bases = (2 * p, 2 * p + 1)
        if first:
            waits[0]()
        qs = [queries_of(g) for g in bases]
        both = jnp.concatenate(qs, axis=0)
        offset = jnp.concatenate([off_ref[pl.ds(g, 1), :] for g in bases], axis=1)
        if first:
            waits[1]()
        scores = dot_nt(k_ref[...], both)
        pos = lax.broadcasted_iota(jnp.int32, scores.shape, 0)
        scores = jnp.where(pos < offset - seq * context, scores, NEG_FILL)
        peak = jnp.max(scores, axis=0, keepdims=True)
        tails = []
        if first:
            waits[2]()
        for i, g in enumerate(bases):
            at = pl.multiple_of(g * band, band)
            keys = sk_ref[pl.ds(at, band)].reshape(band * tail, HD)
            tail_scores = dot_nt(keys, qs[i])
            length = len_ref[pl.ds(g, 1), :] - seq * tail
            tails.append(jnp.where(tail_pos_ref[...] < length, tail_scores, NEG_FILL))
        tail_peak = jnp.concatenate([jnp.max(t, axis=0, keepdims=True) for t in tails], axis=1)
        peak = jnp.maximum(peak, tail_peak)
        weights = jnp.exp2((scores - peak) * SCALE_LOG2).astype(jnp.bfloat16)
        if first:
            waits[3]()
            vt_ref[...] = with_ones(v_ref[...])
            waits[4]()
        sums = jnp.dot(vt_ref[...], weights, preferred_element_type=jnp.float32)
        for i, g in enumerate(bases):
            at = pl.multiple_of(g * band, band)
            own = slice(i * cols, (i + 1) * cols)
            own_peak = peak[:, own]
            tail_weights = jnp.exp2((tails[i] - own_peak) * SCALE_LOG2).astype(jnp.bfloat16)
            values = with_ones(sv_ref[pl.ds(at, band)].reshape(band * tail, HD))
            full = sums[:, own] + jnp.dot(values, tail_weights, preferred_element_type=jnp.float32)
            some = own_peak > 0.5 * NEG_FILL
            total = jnp.where(some, full[HD : HD + 1], 0.0)
            output = jnp.where(some, full[:HD], 0.0).T
            stats = padded(parts_of(own_peak, 3) + parts_of(total, 2), EXTRA)
            out_ref[g] = jnp.concatenate([output, stats], axis=0).astype(jnp.bfloat16)

    pair(0, True)
    pl.loop(1, bands // 2)(lambda p: pair(p, False))


def merged(got_ref):
    count, rows = got_ref.shape[0], got_ref.shape[1] - EXTRA
    stats = [got_ref[s, rows:].astype(jnp.float32) for s in range(count)]
    peaks = [st[0:1] + st[1:2] + st[2:3] for st in stats]
    totals = [st[3:4] + st[4:5] for st in stats]
    peak = functools.reduce(jnp.maximum, peaks)
    factors = [jnp.exp2((p - peak) * SCALE_LOG2) for p in peaks]
    total = sum(f * t for f, t in zip(factors, totals))
    columns = padded(factors + [peak, total], rows).T
    output = sum(
        columns[:, s : s + 1] * got_ref[s, :rows].astype(jnp.float32) for s in range(count)
    )
    return output, peak, total, columns[:, count : count + 1], columns[:, count + 1 : count + 2]


def merge(got_ref, out_ref):
    output, peak, total, _, _ = merged(got_ref)
    stats = padded(parts_of(peak, 3) + parts_of(total, 2), EXTRA)
    message = jnp.concatenate([output, stats], axis=0).astype(jnp.bfloat16)
    for i in range(out_ref.shape[0]):
        out_ref[i] = message


def finish(heads, band, got_ref, q_ref, nk_ref, nv_ref, out_ref):
    output, _, _, peak, total = merged(got_ref)
    own = pl.ds(pl.multiple_of(lax.axis_index("seq") // SIDE * band, band), band)
    tiled = lambda ref: jnp.concatenate([ref[own, :].astype(jnp.float32)] * heads, axis=0)
    query = head_rows(q_ref[own, :], heads).astype(jnp.float32)
    fresh = jnp.sum(query * tiled(nk_ref), axis=1, keepdims=True)
    row_peak = jnp.maximum(peak, fresh)
    factor = jnp.exp2((peak - row_peak) * SCALE_LOG2)
    fresh_factor = jnp.exp2((fresh - row_peak) * SCALE_LOG2)
    numerator = factor * output + fresh_factor * tiled(nv_ref)
    attention = (numerator / (factor * total + fresh_factor)).astype(jnp.bfloat16)
    for i in range(out_ref.shape[0]):
        out_ref[i] = attention


def arrange(gate_ref, up_ref, *outs):
    block = outs[0].shape[2]
    for k in range(QUAD):
        columns = pl.ds(pl.multiple_of((own_place() ^ k) * block, HD), block)
        outs[k][0] = gate_ref[:, columns]
        outs[k][1] = up_ref[:, columns]


def combine(got_ref, residual_ref, gain_ref, hidden_ref, out_ref):
    projected = sum(got_ref[k].astype(jnp.float32) for k in range(got_ref.shape[0]))
    hidden = (residual_ref[...].astype(jnp.float32) + projected).astype(jnp.bfloat16)
    hidden_ref[...] = hidden
    wide = hidden.astype(jnp.float32)
    squares = jnp.sum((wide * wide).T, axis=0, keepdims=True)
    message = jnp.concatenate(
        [wide * gain_ref[...], padded(parts_of(squares, 2), EXTRA)], axis=0
    ).astype(jnp.bfloat16)
    for p in range(QUAD):
        out_ref[p] = message


def gate_up(units, hidden_ref, *refs):
    weights, out_ref = refs[:QUAD], refs[QUAD]
    place = own_place()
    rows = hidden_ref.shape[1] - EXTRA
    totals = [None, None]
    squares = None
    for k in range(QUAD):
        message = hidden_ref[place ^ k]
        hidden = message[:rows]
        extra = message[rows:].astype(jnp.float32)
        row = extra[0:1] + extra[1:2]
        squares = row if squares is None else squares + row
        for i in range(2):
            term = jnp.dot(hidden, weights[k][i], preferred_element_type=jnp.float32)
            totals[i] = term if totals[i] is None else totals[i] + term
    gate, up = [total.T for total in totals]
    extra = padded(parts_of(squares, 2), EXTRA)
    for q in range(BLOCKS):
        part = slice(units * q, units * (q + 1))
        out_ref[q] = jnp.concatenate([gate[part], up[part], extra], axis=0).astype(jnp.bfloat16)


def activate(units, got_ref, out_ref):
    sums = sum(got_ref[q].astype(jnp.float32) for q in range(BLOCKS))
    mean_square = (sums[2 * units : 2 * units + 1] + sums[2 * units + 1 : 2 * units + 2]) / D
    inverse = lax.rsqrt(mean_square + EPSILON)
    gate, up = sums[:units] * inverse, sums[units : 2 * units] * inverse
    activation = gate / (1.0 + jnp.exp(-gate)) * up
    zeros = jnp.zeros((out_ref.shape[0] - units, activation.shape[1]), jnp.float32)
    out_ref[...] = jnp.concatenate([activation, zeros], axis=0).astype(jnp.bfloat16)


def call(kernel, outs, name, *args, hbm=(), scratch=()):
    spec = lambda i: pl.BlockSpec(memory_space=pl.ANY if i in hbm else pltpu.VMEM)
    return pl.pallas_call(
        kernel,
        out_shape=outs,
        in_specs=[spec(i) for i in range(len(args))],
        scratch_shapes=scratch,
        compiler_params=pltpu.CompilerParams(vmem_limit_bytes=(56 if hbm else 32) * MIB),
        name=name,
    )(*args)


def exchange(x, groups):
    return lax.all_to_all(x, "seq", 0, 0, axis_index_groups=groups, tiled=True)


def gather(x, axis, count, groups=None):
    copies = jnp.broadcast_to(x, (count,) + x.shape)
    return lax.all_to_all(copies, axis, 0, 0, axis_index_groups=groups, tiled=True)


def on_device(n_kvh, queries, new_keys, new_values, prefix_keys, prefix_values, suffix_keys,
              suffix_values, prefix_offsets, suffix_lengths, out_weight, residual, norm_gain,
              w_gate, w_up, w_down):
    branches, width = residual.shape
    heads = queries.shape[1] // HD
    bands = SIDE
    band = branches // bands
    rows = heads * band
    hidden_units = w_gate.shape[1]
    units = hidden_units // SIDE**2
    pad = -(-units // 16) * 16
    bf16 = lambda *shape: jax.ShapeDtypeStruct(shape, jnp.bfloat16)
    like = lambda a: pltpu.VMEM(a.shape, a.dtype)
    copies_sem = lambda n: pltpu.SemaphoreType.DMA((n, PIECES))

    message = call(
        functools.partial(attend, bands, band, heads),
        bf16(bands, rows + EXTRA, HD),
        "attend",
        prefix_offsets.reshape(1, branches), suffix_lengths.reshape(1, branches), queries,
        prefix_keys, prefix_values, suffix_keys, suffix_values,
        hbm=(2, 3, 4, 5, 6),
        scratch=[like(queries), like(prefix_keys), like(prefix_values), like(suffix_keys),
                 like(suffix_values),
                 pltpu.VMEM((HD + EXTRA, prefix_keys.shape[0]), jnp.bfloat16),
                 pltpu.VMEM((bands, rows), jnp.int32), pltpu.VMEM((bands, rows), jnp.int32),
                 pltpu.VMEM((band * suffix_keys.shape[1], rows), jnp.int32),
                 copies_sem(5)],
    )
    message, *moved = lax.optimization_barrier((message, w_gate, w_up))
    block = hidden_units // QUAD
    mine = call(arrange, (bf16(2, width, block),) * QUAD, "arrange", *moved)
    swap = lambda x, k: lax.ppermute(
        x, "seq", [(seq_at(p, q), seq_at(p ^ k, q)) for q in range(BLOCKS) for p in range(QUAD)]
    )
    both = [mine[0]] + [swap(mine[k], k) for k in range(1, QUAD)]

    message = call(merge, bf16(SIDE, rows + EXTRA, HD), "merge", exchange(message, Z_GROUPS))
    own = call(
        functools.partial(finish, heads, band), bf16(SIDE, rows, HD), "finish",
        exchange(message, Y_GROUPS), queries, new_keys, new_values,
    )
    gathered = exchange(own, Z_GROUPS)
    attention = (
        gathered.reshape(bands, heads, band, HD).transpose(0, 2, 1, 3).reshape(branches, heads * HD)
    )

    projected = jnp.dot(attention, out_weight, preferred_element_type=jnp.float32)
    hidden, message = call(
        combine, (bf16(branches, width), bf16(QUAD, branches + EXTRA, width)), "combine",
        gather(projected.astype(jnp.bfloat16), "kvh", n_kvh), residual, norm_gain.reshape(1, width),
    )
    message, *both = lax.optimization_barrier((message, *both))
    message = call(
        functools.partial(gate_up, units), bf16(BLOCKS, 2 * units + EXTRA, branches), "gate_up",
        exchange(message, P_GROUPS), *both,
    )
    activation = call(
        functools.partial(activate, units), bf16(pad, branches), "activate",
        exchange(message, Q_GROUPS),
    )[:units]
    activations = gather(activation, "seq", SIDE * SIDE, [SEQ_ORDER]).reshape(hidden_units, branches)
    ffn_part = lax.dot_general(
        activations, w_down, (((0,), (0,)), ((), ())), preferred_element_type=jnp.float32
    )
    terms = gather(ffn_part.astype(jnp.bfloat16), "kvh", n_kvh)
    ffn_sum = jnp.sum(terms.astype(jnp.float32), axis=0)
    mixed = (hidden.astype(jnp.float32) + ffn_sum).astype(jnp.bfloat16)
    return (attention, mixed)


def solution(mesh):
    return jax.shard_map(
        functools.partial(on_device, mesh.shape["kvh"]),
        mesh=mesh,
        in_specs=(
            P(None, "kvh"),
            P(None, "kvh"),
            P(None, "kvh"),
            P("seq", "kvh"),
            P("seq", "kvh"),
            P(None, "seq", "kvh"),
            P(None, "seq", "kvh"),
            P(),
            P(),
            P("kvh", "seq"),
            P(None, "seq"),
            P("seq"),
            P("seq", "kvh"),
            P("seq", "kvh"),
            P("kvh", "seq"),
        ),
        out_specs=(P(None, "kvh"), P(None, "seq")),
        check_vma=False,
    )
```

profile of v0, /device:TPU:1, one launch (start us, length us, event | category | flops | bytes accessed | tf_op | source)
XLA Modules:
  0.0 156.7 jit_solution(9186616282596409696)
XLA Ops:
  0.6 9.6 %attend.1 = bf16[8,144,128]{2,1,0:T(8,128)(2,1)} custom-call(s32[1,128]{1,0:T(1,128)} %bitcast.22, s32[1,128]{1,0:T(1,128)} %bitcast.23, bf16[128,1024]{1,0:T(8,128)(2,1)} %q_ref.1, bf16[2048,128]{1,0:T(8,128)(2,1)} %k_hbm.1, bf16[2048,128]{1,0:T(8,128)(2,1)} %v_hbm.1, bf16[128,16,128]{2,1,0:T(8,128)(2,1)} %sk_hbm.1, bf16[128,16,128]{2,1,0:T(8,128)(2,1)} %sv_hbm.1), custom_call_target="tpu_custom_call" | custom-call | tf_op jit(solution)/shard_map/attend/pallas_call | solution.py:264
  10.3 21.7 %all_to_all.40.got_ref = bf16[8,144,128]{2,1,0:T(8,128)(2,1)S(1)} all-to-all(bf16[8,144,128]{2,1,0:T(8,128)(2,1)} %attend.1), channel_id=1, replica_groups={{0,64,128,192,256,320,384,448},{8,72,136,200,264,328,392,456},{16,80,14..., dimensions={0} | all-to-all | bytes 589824 | tf_op jit(solution)/shard_map/all_to_all | solution.py:275
  32.0 0.4 merge.1
  32.4 16.4 %all_to_all.41.got_ref = bf16[8,144,128]{2,1,0:T(8,128)(2,1)S(1)} all-to-all(bf16[8,144,128]{2,1,0:T(8,128)(2,1)S(1)} %merge.1), channel_id=1, replica_groups={{0,8,16,24,32,40,48,56},{64,72,80,88,96,104,112,120},{128,136,144,152,1..., dimensions={0} | all-to-all | bytes 589824 | tf_op jit(solution)/shard_map/all_to_all | solution.py:275
  48.9 1.3 finish.1
  50.2 4.0 %all-to-all-start.2 = ((bf16[8,128,128]{2,1,0:T(8,128)(2,1)}), bf16[8,128,128]{2,1,0:T(8,128)(2,1)S(1)}, u32[]{:S(2)}, u32[]{:S(2)}) async-start(bf16[8,128,128]{2,1,0:T(8,128)(2,1)} %finish.1), calls=%async_computation.2 | async-start | bytes 524288 | tf_op jit(solution)/shard_map/all_to_all | solution.py:275
  54.3 1.2 arrange.1
  55.5 1.9 %collective-permute-start = (bf16[2,128,896]{2,1,0:T(8,128)(2,1)}, bf16[2,128,896]{2,1,0:T(8,128)(2,1)S(1)}, u32[]{:S(2)}, u32[]{:S(2)}) collective-permute-start(bf16[2,128,896]{2,1,0:T(8,128)(2,1)} %get-tuple-element.22), channel_id=1, source_target_pairs={{0,8},{8,0},{64,72},{72,64},{16,24},{24,16},{80,88},{88,80},{32,40... | collective-permute-start | bytes 1376264 | tf_op jit(solution)/shard_map/ppermute | solution.py:315
  57.4 3.4 %collective-permute-start.1 = (bf16[2,128,896]{2,1,0:T(8,128)(2,1)}, bf16[2,128,896]{2,1,0:T(8,128)(2,1)S(1)}, u32[]{:S(2)}, u32[]{:S(2)}) collective-permute-start(bf16[2,128,896]{2,1,0:T(8,128)(2,1)} %get-tuple-element.23), channel_id=1, source_target_pairs={{0,64},{8,72},{64,0},{72,8},{16,80},{24,88},{80,16},{88,24},{32,96... | collective-permute-start | bytes 1376264 | tf_op jit(solution)/shard_map/ppermute | solution.py:315
  60.8 3.1 %collective-permute-start.2 = (bf16[2,128,896]{2,1,0:T(8,128)(2,1)}, bf16[2,128,896]{2,1,0:T(8,128)(2,1)S(1)}, u32[]{:S(2)}, u32[]{:S(2)}) collective-permute-start(bf16[2,128,896]{2,1,0:T(8,128)(2,1)} %get-tuple-element.24), channel_id=1, source_target_pairs={{0,72},{8,64},{64,8},{72,0},{16,88},{24,80},{80,24},{88,16},{32,10... | collective-permute-start | bytes 1376264 | tf_op jit(solution)/shard_map/ppermute | solution.py:315
  64.0 0.9 copy-done.9
  64.9 0.2 convolution_convert_fusion.1
  65.2 15.2 %all_to_all.42.got_ref = bf16[8,128,128]{2,1,0:T(8,128)(2,1)S(1)} all-to-all(bf16[8,128,128]{2,1,0:T(8,128)(2,1)S(1)} %broadcast_in_dim.9), channel_id=1, replica_groups=mesh['seq'=64,'kvh'=8] {'kvh'}, dimensions={0} | all-to-all | bytes 524288 | tf_op jit(solution)/shard_map/all_to_all | solution.py:280
  80.4 0.7 copy-done.7
  81.0 0.1 combine.1
  81.2 6.7 %all_to_all.43.hidden_ref = bf16[4,144,128]{2,1,0:T(8,128)(2,1)S(1)} all-to-all(bf16[4,144,128]{2,1,0:T(8,128)(2,1)S(1)} %get-tuple-element.25), channel_id=1, replica_groups={{0,8,64,72},{16,24,80,88},{32,40,96,104},{48,56,112,120},{128,136,192,2..., dimensions={0} | all-to-all | bytes 294912 | tf_op jit(solution)/shard_map/all_to_all | solution.py:275
  87.9 0.7 gate_up.1
  88.6 22.1 %all_to_all.44.got_ref = bf16[16,128,128]{2,1,0:T(8,128)(2,1)S(1)} all-to-all(bf16[16,128,128]{2,1,0:T(8,128)(2,1)S(1)} %gate_up.1), channel_id=1, replica_groups={{0,16,32,48,128,144,160,176,256,272,288,304,384,400,416,432},{8,24,40,5..., dimensions={0} | all-to-all | bytes 1048576 | tf_op jit(solution)/shard_map/all_to_all | solution.py:275
  110.7 0.1 activate.1
  110.8 0.1 broadcast_in_dim.10
  110.9 26.3 %all_to_all.45 = bf16[64,56,128]{2,1,0:T(8,128)(2,1)S(1)} all-to-all(bf16[64,56,128]{2,1,0:T(8,128)(2,1)S(1)} %broadcast_in_dim.10), channel_id=1, replica_groups={{0,16,32,48,128,144,160,176,256,272,288,304,384,400,416,432,8,24,40,56,..., dimensions={0} | all-to-all | bytes 1835008 | tf_op jit(solution)/shard_map/all_to_all | solution.py:280
  137.2 0.4 convolution_convert_fusion
  137.7 18.4 %all_to_all.46 = bf16[8,128,128]{2,1,0:T(8,128)(2,1)S(1)} all-to-all(bf16[8,128,128]{2,1,0:T(8,128)(2,1)S(1)} %broadcast_in_dim.11), channel_id=1, replica_groups=mesh['seq'=64,'kvh'=8] {'kvh'}, dimensions={0} | all-to-all | bytes 524288 | tf_op jit(solution)/shard_map/all_to_all | solution.py:280
  156.1 0.6 add_convert_fusion
  (28 shorter events, 0.3 us)
Async XLA Ops:
  0.6 136.6 %copy-start = (bf16[3584,128]{1,0:T(8,128)(2,1)S(1)}, bf16[3584,128]{1,0:T(8,128)(2,1)}, u32[]{:S(2)}) copy-start(bf16[3584,128]{1,0:T(8,128)(2,1)} %param.29) | copy-start | bytes 2752516
  10.3 38.6 %copy-start.4 = (bf16[128,128]{1,0:T(8,128)(2,1)S(1)}, bf16[128,128]{1,0:T(8,128)(2,1)}, u32[]{:S(2)}) copy-start(bf16[128,128]{1,0:T(8,128)(2,1)} %nk_ref.1) | copy-start | bytes 98308
  10.3 38.6 %copy-start.5 = (bf16[128,128]{1,0:T(8,128)(2,1)S(1)}, bf16[128,128]{1,0:T(8,128)(2,1)}, u32[]{:S(2)}) copy-start(bf16[128,128]{1,0:T(8,128)(2,1)} %nv_ref.1) | copy-start | bytes 98308
  32.0 22.2 %copy-start.3 = (bf16[128,3584]{1,0:T(8,128)(2,1)S(1)}, bf16[128,3584]{1,0:T(8,128)(2,1)}, u32[]{:S(2)}) copy-start(bf16[128,3584]{1,0:T(8,128)(2,1)} %up_ref) | copy-start | bytes 2752516
  32.4 16.5 %copy-start.1 = (bf16[128,1024]{1,0:T(8,128)(2,1)S(1)}, bf16[128,1024]{1,0:T(8,128)(2,1)}, u32[]{:S(2)}) copy-start(bf16[128,1024]{1,0:T(8,128)(2,1)} %q_ref.1) | copy-start | bytes 786436
  32.4 21.8 %copy-start.2 = (bf16[128,3584]{1,0:T(8,128)(2,1)S(1)}, bf16[128,3584]{1,0:T(8,128)(2,1)}, u32[]{:S(2)}) copy-start(bf16[128,3584]{1,0:T(8,128)(2,1)} %gate_ref) | copy-start | bytes 2752516
  50.2 13.7 %all-to-all-start.2 = ((bf16[8,128,128]{2,1,0:T(8,128)(2,1)}), bf16[8,128,128]{2,1,0:T(8,128)(2,1)S(1)}, u32[]{:S(2)}, u32[]{:S(2)}) async-start(bf16[8,128,128]{2,1,0:T(8,128)(2,1)} %finish.1), calls=%async_computation.2 | async-start | bytes 524288 | tf_op jit(solution)/shard_map/all_to_all | solution.py:275
  55.5 25.7 %collective-permute-start = (bf16[2,128,896]{2,1,0:T(8,128)(2,1)}, bf16[2,128,896]{2,1,0:T(8,128)(2,1)S(1)}, u32[]{:S(2)}, u32[]{:S(2)}) collective-permute-start(bf16[2,128,896]{2,1,0:T(8,128)(2,1)} %get-tuple-element.22), channel_id=1, source_target_pairs={{0,8},{8,0},{64,72},{72,64},{16,24},{24,16},{80,88},{88,80},{32,40... | collective-permute-start | bytes 1376264 | tf_op jit(solution)/shard_map/ppermute | solution.py:315
  57.4 23.8 %collective-permute-start.1 = (bf16[2,128,896]{2,1,0:T(8,128)(2,1)}, bf16[2,128,896]{2,1,0:T(8,128)(2,1)S(1)}, u32[]{:S(2)}, u32[]{:S(2)}) collective-permute-start(bf16[2,128,896]{2,1,0:T(8,128)(2,1)} %get-tuple-element.23), channel_id=1, source_target_pairs={{0,64},{8,72},{64,0},{72,8},{16,80},{24,88},{80,16},{88,24},{32,96... | collective-permute-start | bytes 1376264 | tf_op jit(solution)/shard_map/ppermute | solution.py:315
  60.8 20.4 %collective-permute-start.2 = (bf16[2,128,896]{2,1,0:T(8,128)(2,1)}, bf16[2,128,896]{2,1,0:T(8,128)(2,1)S(1)}, u32[]{:S(2)}, u32[]{:S(2)}) collective-permute-start(bf16[2,128,896]{2,1,0:T(8,128)(2,1)} %get-tuple-element.24), channel_id=1, source_target_pairs={{0,72},{8,64},{64,8},{72,0},{16,88},{24,80},{80,24},{88,16},{32,10... | collective-permute-start | bytes 1376264 | tf_op jit(solution)/shard_map/ppermute | solution.py:315
  64.0 1.0 copy-start.9
  64.0 1.1 copy-start.8
  65.2 15.2 %copy-start.6 = (bf16[128,128]{1,0:T(8,128)(2,1)S(1)}, bf16[128,128]{1,0:T(8,128)(2,1)}, u32[]{:S(2)}) copy-start(bf16[128,128]{1,0:T(8,128)(2,1)} %residual_ref.1) | copy-start | bytes 98308
  80.4 0.7 copy-start.7
where the time goes:
time: 158 us; the launch traced here: 157 us
  blocking collectives  127 us (80%)
  Pallas kernels  13.5 us (9%)
  starting transfers between devices  12.4 us (8%)
  local copies, waits for them, and re-layouts  1.9 us (1%)
    all_to_all x4, blocking collectives, exchange(): return lax.all_to_all(x, 'seq', 0, 0, axis_index_groups=groups, tiled=True)  67 us
    all_to_all x3, blocking collectives, gather(): lax.all_to_all(copies, axis, 0, 0, axis_index_groups=groups, tiled=True)  59.8 us
    pallas_call x7, Pallas kernels, call(): pl.pallas_call(kernel, out_shape=outs, in_specs=[spec(i) for i in range(l...  13.5 us
    ppermute x3, starting transfers between devices, on_device(): lax.ppermute(x, 'seq', [(seq_at(p, q), seq_at(p ^ k, q)) for q in range(B...  8.36 us
    all_to_all x1, starting transfers between devices, exchange(): return lax.all_to_all(x, 'seq', 0, 0, axis_index_groups=groups, tiled=True)  4.04 us
  transfers between devices with their start and end apart: 4, of which 0 were waited for; matrix products, arithmetic and copies ran while one was open for 0% of the time, Pallas kernels for 1%

commit v1 on v0

--- a/solution.py
+++ b/solution.py
@@ -11,8 +11,6 @@
 HD = 128
 D = 8192
 SIDE = 8
-Z_GROUPS = [[z * SIDE + y for z in range(SIDE)] for y in range(SIDE)]
-Y_GROUPS = [[z * SIDE + y for y in range(SIDE)] for z in range(SIDE)]
 QUAD = 4
 BLOCKS = SIDE * SIDE // QUAD
 
@@ -27,6 +25,7 @@
 NEG_FILL = -1e30
 EPSILON = 1e-05
 SCALE_LOG2 = math.log2(math.e) / math.sqrt(HD)
+STATS = 8
 EXTRA = 16
 PIECES = 4
 MIB = 2**20
@@ -103,7 +102,7 @@
 
 def attend(bands, band, heads, offsets_ref, lengths_ref, q_hbm, k_hbm, v_hbm, sk_hbm, sv_hbm, out_ref,
            q_ref, k_ref, v_ref, sk_ref, sv_ref, vt_ref, off_ref, len_ref, tail_pos_ref,
-           sems):
+           weight_ref, tail_weight_ref, peak_ref, sems):
     context = k_ref.shape[0]
     tail = sk_ref.shape[1]
     cols = heads * band
@@ -121,7 +120,7 @@
     def queries_of(g):
         return head_rows(q_ref[pl.ds(pl.multiple_of(g * band, band), band), :], heads)
 
-    def pair(p, first):
+    def weigh(p, first):
         bases = (2 * p, 2 * p + 1)
         if first:
             waits[0]()
@@ -145,62 +144,61 @@
             tails.append(jnp.where(tail_pos_ref[...] < length, tail_scores, NEG_FILL))
         tail_peak = jnp.concatenate([jnp.max(t, axis=0, keepdims=True) for t in tails], axis=1)
         peak = jnp.maximum(peak, tail_peak)
-        weights = jnp.exp2((scores - peak) * SCALE_LOG2).astype(jnp.bfloat16)
-        if first:
-            waits[3]()
-            vt_ref[...] = with_ones(v_ref[...])
-            waits[4]()
-        sums = jnp.dot(vt_ref[...], weights, preferred_element_type=jnp.float32)
+        weight_ref[p] = jnp.exp2((scores - peak) * SCALE_LOG2).astype(jnp.bfloat16)
         for i, g in enumerate(bases):
+            own_peak = peak[:, i * cols : (i + 1) * cols]
+            peak_ref[pl.ds(g, 1), :] = own_peak
+            tail_weight_ref[g] = jnp.exp2((tails[i] - own_peak) * SCALE_LOG2).astype(jnp.bfloat16)
+
+    def add_up(p):
+        sums = jnp.dot(vt_ref[...], weight_ref[p], preferred_element_type=jnp.float32)
+        for i, g in enumerate((2 * p, 2 * p + 1)):
             at = pl.multiple_of(g * band, band)
-            own = slice(i * cols, (i + 1) * cols)
-            own_peak = peak[:, own]
-            tail_weights = jnp.exp2((tails[i] - own_peak) * SCALE_LOG2).astype(jnp.bfloat16)
             values = with_ones(sv_ref[pl.ds(at, band)].reshape(band * tail, HD))
-            full = sums[:, own] + jnp.dot(values, tail_weights, preferred_element_type=jnp.float32)
+            full = sums[:, i * cols : (i + 1) * cols] + jnp.dot(
+                values, tail_weight_ref[g], preferred_element_type=jnp.float32
+            )
+            own_peak = peak_ref[pl.ds(g, 1), :]
             some = own_peak > 0.5 * NEG_FILL
             total = jnp.where(some, full[HD : HD + 1], 0.0)
             output = jnp.where(some, full[:HD], 0.0).T
-            stats = padded(parts_of(own_peak, 3) + parts_of(total, 2), EXTRA)
-            out_ref[g] = jnp.concatenate([output, stats], axis=0).astype(jnp.bfloat16)
-
-    pair(0, True)
-    pl.loop(1, bands // 2)(lambda p: pair(p, False))
-
-
-def merged(got_ref):
-    count, rows = got_ref.shape[0], got_ref.shape[1] - EXTRA
-    stats = [got_ref[s, rows:].astype(jnp.float32) for s in range(count)]
-    peaks = [st[0:1] + st[1:2] + st[2:3] for st in stats]
-    totals = [st[3:4] + st[4:5] for st in stats]
-    peak = functools.reduce(jnp.maximum, peaks)
-    factors = [jnp.exp2((p - peak) * SCALE_LOG2) for p in peaks]
-    total = sum(f * t for f, t in zip(factors, totals))
-    columns = padded(factors + [peak, total], rows).T
-    output = sum(
-        columns[:, s : s + 1] * got_ref[s, :rows].astype(jnp.float32) for s in range(count)
-    )
-    return output, peak, total, columns[:, count : count + 1], columns[:, count + 1 : count + 2]
-
-
-def merge(got_ref, out_ref):
-    output, peak, total, _, _ = merged(got_ref)
-    stats = padded(parts_of(peak, 3) + parts_of(total, 2), EXTRA)
-    message = jnp.concatenate([output, stats], axis=0).astype(jnp.bfloat16)
-    for i in range(out_ref.shape[0]):
-        out_ref[i] = message
-
-
-def finish(heads, band, got_ref, q_ref, nk_ref, nv_ref, out_ref):
-    output, _, _, peak, total = merged(got_ref)
-    own = pl.ds(pl.multiple_of(lax.axis_index("seq") // SIDE * band, band), band)
-    tiled = lambda ref: jnp.concatenate([ref[own, :].astype(jnp.float32)] * heads, axis=0)
-    query = head_rows(q_ref[own, :], heads).astype(jnp.float32)
-    fresh = jnp.sum(query * tiled(nk_ref), axis=1, keepdims=True)
+            stats = padded(parts_of(own_peak, 3) + parts_of(total, 2), STATS)
+            for h in range(heads):
+                message = jnp.concatenate([output[h * band : (h + 1) * band], stats], axis=0)
+                out_ref[g * heads + h] = message.astype(jnp.bfloat16)
+
+    weigh(0, True)
+    pl.loop(1, bands // 2)(lambda p: weigh(p, False))
+    waits[3]()
+    vt_ref[...] = with_ones(v_ref[...])
+    waits[4]()
+    pl.loop(0, bands // 2)(add_up)
+
+
+def finish(heads, band, got_ref, q_ref, nk_ref, nv_ref, out_ref, columns_ref):
+    count = got_ref.shape[0]
+    seq = lax.axis_index("seq")
+    own_band, own_head = seq // heads, seq % heads
+    got = got_ref[...].astype(jnp.float32)
+    stats = got[:, band:]
+    kind = lax.broadcasted_iota(jnp.int32, stats.shape, 1)
+    peaks = jnp.sum(jnp.where(kind < 3, stats, 0.0), axis=1)
+    totals = jnp.sum(jnp.where(kind >= 3, stats, 0.0), axis=1)
+    peak = jnp.max(peaks, axis=0, keepdims=True)
+    factors = jnp.exp2((peaks - peak) * SCALE_LOG2)
+    total = jnp.sum(factors * totals, axis=0, keepdims=True)
+    zeros = jnp.zeros((peaks.shape[1] - count - 2, peaks.shape[1]), jnp.float32)
+    columns_ref[...] = jnp.concatenate([factors, peak, total, zeros], axis=0).T
+    columns = columns_ref[pl.ds(pl.multiple_of(own_head * band, band), band), :]
+    output = sum(columns[:, s : s + 1] * got[s, :band] for s in range(count))
+    peak, total = columns[:, count : count + 1], columns[:, count + 1 : count + 2]
+    own = pl.ds(pl.multiple_of(own_band * band, band), band)
+    query = q_ref[own, pl.ds(pl.multiple_of(own_head * HD, HD), HD)].astype(jnp.float32)
+    fresh = jnp.sum(query * nk_ref[own, :].astype(jnp.float32), axis=1, keepdims=True)
     row_peak = jnp.maximum(peak, fresh)
     factor = jnp.exp2((peak - row_peak) * SCALE_LOG2)
     fresh_factor = jnp.exp2((fresh - row_peak) * SCALE_LOG2)
-    numerator = factor * output + fresh_factor * tiled(nv_ref)
+    numerator = factor * output + fresh_factor * nv_ref[own, :].astype(jnp.float32)
     attention = (numerator / (factor * total + fresh_factor)).astype(jnp.bfloat16)
     for i in range(out_ref.shape[0]):
         out_ref[i] = attention
@@ -243,7 +241,7 @@
             term = jnp.dot(hidden, weights[k][i], preferred_element_type=jnp.float32)
             totals[i] = term if totals[i] is None else totals[i] + term
     gate, up = [total.T for total in totals]
-    extra = padded(parts_of(squares, 2), EXTRA)
+    extra = padded(parts_of(squares, 2), STATS)
     for q in range(BLOCKS):
         part = slice(units * q, units * (q + 1))
         out_ref[q] = jnp.concatenate([gate[part], up[part], extra], axis=0).astype(jnp.bfloat16)
@@ -288,6 +286,7 @@
     bands = SIDE
     band = branches // bands
     rows = heads * band
+    tail_rows = band * suffix_keys.shape[1]
     hidden_units = w_gate.shape[1]
     units = hidden_units // SIDE**2
     pad = -(-units // 16) * 16
@@ -297,7 +296,7 @@
 
     message = call(
         functools.partial(attend, bands, band, heads),
-        bf16(bands, rows + EXTRA, HD),
+        bf16(SIDE * SIDE, band + STATS, HD),
         "attend",
         prefix_offsets.reshape(1, branches), suffix_lengths.reshape(1, branches), queries,
         prefix_keys, prefix_values, suffix_keys, suffix_values,
@@ -306,7 +305,10 @@
                  like(suffix_values),
                  pltpu.VMEM((HD + EXTRA, prefix_keys.shape[0]), jnp.bfloat16),
                  pltpu.VMEM((bands, rows), jnp.int32), pltpu.VMEM((bands, rows), jnp.int32),
-                 pltpu.VMEM((band * suffix_keys.shape[1], rows), jnp.int32),
+                 pltpu.VMEM((tail_rows, rows), jnp.int32),
+                 pltpu.VMEM((bands // 2, prefix_keys.shape[0], 2 * rows), jnp.bfloat16),
+                 pltpu.VMEM((bands, tail_rows, rows), jnp.bfloat16),
+                 pltpu.VMEM((bands, rows), jnp.float32),
                  copies_sem(5)],
     )
     message, *moved = lax.optimization_barrier((message, w_gate, w_up))
@@ -317,12 +319,12 @@
     )
     both = [mine[0]] + [swap(mine[k], k) for k in range(1, QUAD)]
 
-    message = call(merge, bf16(SIDE, rows + EXTRA, HD), "merge", exchange(message, Z_GROUPS))
     own = call(
-        functools.partial(finish, heads, band), bf16(SIDE, rows, HD), "finish",
-        exchange(message, Y_GROUPS), queries, new_keys, new_values,
-    )
-    gathered = exchange(own, Z_GROUPS)
+        functools.partial(finish, heads, band), bf16(SIDE * SIDE, band, HD), "finish",
+        exchange(message, None), queries, new_keys, new_values,
+        scratch=[pltpu.VMEM((rows, HD), jnp.float32)],
+    )
+    gathered = exchange(own, None)
     attention = (
         gathered.reshape(bands, heads, band, HD).transpose(0, 2, 1, 3).reshape(branches, heads * HD)
     )
@@ -334,7 +336,7 @@
     )
     message, *both = lax.optimization_barrier((message, *both))
     message = call(
-        functools.partial(gate_up, units), bf16(BLOCKS, 2 * units + EXTRA, branches), "gate_up",
+        functools.partial(gate_up, units), bf16(BLOCKS, 2 * units + STATS, branches), "gate_up",
         exchange(message, P_GROUPS), *both,
     )
     activation = call(

time: 158 us -> 161 us (1.019)
  waiting for transfers between devices: 0.01 us -> 2.89 us
  starting transfers between devices: 12.4 us -> 14.4 us
    all_to_all x3, blocking collectives: 59.8 us -> 62.7 us  [gather(): lax.all_to_all(copies, axis, 0, 0, axis_index_groups=groups, tiled=True)]
    all_to_all x1, waiting for transfers between devices: 0.01 us -> 2.88 us  [exchange(): return lax.all_to_all(x, 'seq', 0, 0, axis_index_groups=groups, tiled=True)]
    all_to_all x4 -> x3, blocking collectives: 67 us -> 64.3 us  [exchange(): return lax.all_to_all(x, 'seq', 0, 0, axis_index_groups=groups, tiled=True)]
    all_to_all x1, starting transfers between devices: 4.04 us -> 6 us  [exchange(): return lax.all_to_all(x, 'seq', 0, 0, axis_index_groups=groups, tiled=True)]
    pallas_call x7 -> x6, Pallas kernels: 13.5 us -> 12.2 us  [call(): pl.pallas_call(kernel, out_shape=outs, in_specs=[spec(i) for i in range(l...]
  transfers between devices with their start and end apart: 4 -> 4, of which waited for: 0 -> 1; matrix products, arithmetic and copies ran while one was open for 0% -> 0% of each run, Pallas kernels for 1% -> 1%
where the time goes in v1:
time: 161 us
  blocking collectives  127 us (79%)
  starting transfers between devices  14.4 us (9%)
  Pallas kernels  12.2 us (8%)
  waiting for transfers between devices  2.89 us (2%)
  local copies, waits for them, and re-layouts  1.89 us (1%)
    all_to_all x3, blocking collectives, exchange(): return lax.all_to_all(x, 'seq', 0, 0, axis_index_groups=groups, tiled=True)  64.3 us
    all_to_all x3, blocking collectives, gather(): lax.all_to_all(copies, axis, 0, 0, axis_index_groups=groups, tiled=True)  62.7 us
    pallas_call x6, Pallas kernels, call(): pl.pallas_call(kernel, out_shape=outs, in_specs=[spec(i) for i in range(l...  12.2 us
    ppermute x3, starting transfers between devices, on_device(): lax.ppermute(x, 'seq', [(seq_at(p, q), seq_at(p ^ k, q)) for q in range(B...  8.36 us
    all_to_all x1, starting transfers between devices, exchange(): return lax.all_to_all(x, 'seq', 0, 0, axis_index_groups=groups, tiled=True)  6 us
  transfers between devices with their start and end apart: 4, of which 1 were waited for; matrix products, arithmetic and copies ran while one was open for 0% of the time, Pallas kernels for 1%

profile of v1, /device:TPU:1, one launch (start us, length us, event | category | flops | bytes accessed | tf_op | source)
XLA Modules:
  0.0 160.6 jit_solution(8921643007014218768)
XLA Ops:
  0.7 8.7 %attend.1 = bf16[64,24,128]{2,1,0:T(8,128)(2,1)} custom-call(s32[1,128]{1,0:T(1,128)} %bitcast.22, s32[1,128]{1,0:T(1,128)} %bitcast.23, bf16[128,1024]{1,0:T(8,128)(2,1)} %q_ref.1, bf16[2048,128]{1,0:T(8,128)(2,1)} %k_hbm.1, bf16[2048,128]{1,0:T(8,128)(2,1)} %v_hbm.1, bf16[128,16,128]{2,1,0:T(8,128)(2,1)} %sk_hbm.1, bf16[128,16,128]{2,1,0:T(8,128)(2,1)} %sv_hbm.1), custom_call_target="tpu_custom_call" | custom-call | tf_op jit(solution)/shard_map/attend/pallas_call | solution.py:262
  9.4 32.3 %all_to_all.35.got_ref = bf16[64,24,128]{2,1,0:T(8,128)(2,1)S(1)} all-to-all(bf16[64,24,128]{2,1,0:T(8,128)(2,1)} %attend.1), channel_id=1, replica_groups=mesh['seq'=64,'kvh'=8] {'seq'}, dimensions={0} | all-to-all | bytes 786432 | tf_op jit(solution)/shard_map/all_to_all | solution.py:273
  41.8 1.4 finish.1
  43.1 6.0 %all-to-all-start.1 = ((bf16[64,16,128]{2,1,0:T(8,128)(2,1)}), bf16[64,16,128]{2,1,0:T(8,128)(2,1)S(1)}, u32[]{:S(2)}, u32[]{:S(2)}) async-start(bf16[64,16,128]{2,1,0:T(8,128)(2,1)} %finish.1), calls=%async_computation.1 | async-start | bytes 524288 | tf_op jit(solution)/shard_map/all_to_all | solution.py:273
  49.2 1.2 arrange.1
  50.4 2.9 %collective-permute-start = (bf16[2,128,896]{2,1,0:T(8,128)(2,1)}, bf16[2,128,896]{2,1,0:T(8,128)(2,1)S(1)}, u32[]{:S(2)}, u32[]{:S(2)}) collective-permute-start(bf16[2,128,896]{2,1,0:T(8,128)(2,1)} %get-tuple-element.22), channel_id=1, source_target_pairs={{0,8},{8,0},{64,72},{72,64},{16,24},{24,16},{80,88},{88,80},{32,40... | collective-permute-start | bytes 1376264 | tf_op jit(solution)/shard_map/ppermute | solution.py:317
  53.3 3.1 %collective-permute-start.1 = (bf16[2,128,896]{2,1,0:T(8,128)(2,1)}, bf16[2,128,896]{2,1,0:T(8,128)(2,1)S(1)}, u32[]{:S(2)}, u32[]{:S(2)}) collective-permute-start(bf16[2,128,896]{2,1,0:T(8,128)(2,1)} %get-tuple-element.23), channel_id=1, source_target_pairs={{0,64},{8,72},{64,0},{72,8},{16,80},{24,88},{80,16},{88,24},{32,96... | collective-permute-start | bytes 1376264 | tf_op jit(solution)/shard_map/ppermute | solution.py:317
  56.4 2.4 %collective-permute-start.2 = (bf16[2,128,896]{2,1,0:T(8,128)(2,1)}, bf16[2,128,896]{2,1,0:T(8,128)(2,1)S(1)}, u32[]{:S(2)}, u32[]{:S(2)}) collective-permute-start(bf16[2,128,896]{2,1,0:T(8,128)(2,1)} %get-tuple-element.24), channel_id=1, source_target_pairs={{0,72},{8,64},{64,8},{72,0},{16,88},{24,80},{80,24},{88,16},{32,10... | collective-permute-start | bytes 1376264 | tf_op jit(solution)/shard_map/ppermute | solution.py:317
  58.8 2.9 %all-to-all-done.1 = bf16[64,16,128]{2,1,0:T(8,128)(2,1)S(1)} async-done(((bf16[64,16,128]{2,1,0:T(8,128)(2,1)}), bf16[64,16,128]{2,1,0:T(8,128)(2,1)S(1)}, u32[]{:S(2)}, u32[]{:S(2)}) %all-to-all-start.1) | async-done | bytes 262176 | tf_op jit(solution)/shard_map/all_to_all | solution.py:273
  61.6 0.1 copy.18
  61.8 0.9 copy-done.9
  62.7 0.2 convolution_convert_fusion.1
  63.0 14.8 %all_to_all.36.got_ref = bf16[8,128,128]{2,1,0:T(8,128)(2,1)S(1)} all-to-all(bf16[8,128,128]{2,1,0:T(8,128)(2,1)S(1)} %broadcast_in_dim.9), channel_id=1, replica_groups=mesh['seq'=64,'kvh'=8] {'kvh'}, dimensions={0} | all-to-all | bytes 524288 | tf_op jit(solution)/shard_map/all_to_all | solution.py:278
  77.7 0.7 copy-done.7
  78.4 0.1 combine.1
  78.6 6.6 %all_to_all.37.hidden_ref = bf16[4,144,128]{2,1,0:T(8,128)(2,1)S(1)} all-to-all(bf16[4,144,128]{2,1,0:T(8,128)(2,1)S(1)} %get-tuple-element.25), channel_id=1, replica_groups={{0,8,64,72},{16,24,80,88},{32,40,96,104},{48,56,112,120},{128,136,192,2..., dimensions={0} | all-to-all | bytes 294912 | tf_op jit(solution)/shard_map/all_to_all | solution.py:273
  85.2 0.7 gate_up.1
  85.9 25.3 %all_to_all.38.got_ref = bf16[16,120,128]{2,1,0:T(8,128)(2,1)S(1)} all-to-all(bf16[16,120,128]{2,1,0:T(8,128)(2,1)S(1)} %gate_up.1), channel_id=1, replica_groups={{0,16,32,48,128,144,160,176,256,272,288,304,384,400,416,432},{8,24,40,5..., dimensions={0} | all-to-all | bytes 983040 | tf_op jit(solution)/shard_map/all_to_all | solution.py:273
  111.2 0.1 activate.1
  111.3 0.1 broadcast_in_dim.10
  111.4 33.3 %all_to_all.39 = bf16[64,56,128]{2,1,0:T(8,128)(2,1)S(1)} all-to-all(bf16[64,56,128]{2,1,0:T(8,128)(2,1)S(1)} %broadcast_in_dim.10), channel_id=1, replica_groups={{0,16,32,48,128,144,160,176,256,272,288,304,384,400,416,432,8,24,40,56,..., dimensions={0} | all-to-all | bytes 1835008 | tf_op jit(solution)/shard_map/all_to_all | solution.py:278
  144.8 0.4 convolution_convert_fusion
  145.2 14.6 %all_to_all.40 = bf16[8,128,128]{2,1,0:T(8,128)(2,1)S(1)} all-to-all(bf16[8,128,128]{2,1,0:T(8,128)(2,1)S(1)} %broadcast_in_dim.11), channel_id=1, replica_groups=mesh['seq'=64,'kvh'=8] {'kvh'}, dimensions={0} | all-to-all | bytes 524288 | tf_op jit(solution)/shard_map/all_to_all | solution.py:278
  159.9 0.6 add_convert_fusion
  (26 shorter events, 0.2 us)
Async XLA Ops:
  0.6 144.1 %copy-start = (bf16[3584,128]{1,0:T(8,128)(2,1)S(1)}, bf16[3584,128]{1,0:T(8,128)(2,1)}, u32[]{:S(2)}) copy-start(bf16[3584,128]{1,0:T(8,128)(2,1)} %param.29) | copy-start | bytes 2752516
  0.6 41.1 %copy-start.4 = (bf16[128,128]{1,0:T(8,128)(2,1)S(1)}, bf16[128,128]{1,0:T(8,128)(2,1)}, u32[]{:S(2)}) copy-start(bf16[128,128]{1,0:T(8,128)(2,1)} %nk_ref.1) | copy-start | bytes 98308
  0.7 41.1 %copy-start.5 = (bf16[128,128]{1,0:T(8,128)(2,1)S(1)}, bf16[128,128]{1,0:T(8,128)(2,1)}, u32[]{:S(2)}) copy-start(bf16[128,128]{1,0:T(8,128)(2,1)} %nv_ref.1) | copy-start | bytes 98308
  9.4 32.4 %copy-start.1 = (bf16[128,1024]{1,0:T(8,128)(2,1)S(1)}, bf16[128,1024]{1,0:T(8,128)(2,1)}, u32[]{:S(2)}) copy-start(bf16[128,1024]{1,0:T(8,128)(2,1)} %q_ref.1) | copy-start | bytes 786436
  9.4 39.7 %copy-start.3 = (bf16[128,3584]{1,0:T(8,128)(2,1)S(1)}, bf16[128,3584]{1,0:T(8,128)(2,1)}, u32[]{:S(2)}) copy-start(bf16[128,3584]{1,0:T(8,128)(2,1)} %up_ref) | copy-start | bytes 2752516
  41.8 7.4 %copy-start.2 = (bf16[128,3584]{1,0:T(8,128)(2,1)S(1)}, bf16[128,3584]{1,0:T(8,128)(2,1)}, u32[]{:S(2)}) copy-start(bf16[128,3584]{1,0:T(8,128)(2,1)} %gate_ref) | copy-start | bytes 2752516
  43.1 18.5 %all-to-all-start.1 = ((bf16[64,16,128]{2,1,0:T(8,128)(2,1)}), bf16[64,16,128]{2,1,0:T(8,128)(2,1)S(1)}, u32[]{:S(2)}, u32[]{:S(2)}) async-start(bf16[64,16,128]{2,1,0:T(8,128)(2,1)} %finish.1), calls=%async_computation.1 | async-start | bytes 524288 | tf_op jit(solution)/shard_map/all_to_all | solution.py:273
  50.4 28.1 %collective-permute-start = (bf16[2,128,896]{2,1,0:T(8,128)(2,1)}, bf16[2,128,896]{2,1,0:T(8,128)(2,1)S(1)}, u32[]{:S(2)}, u32[]{:S(2)}) collective-permute-start(bf16[2,128,896]{2,1,0:T(8,128)(2,1)} %get-tuple-element.22), channel_id=1, source_target_pairs={{0,8},{8,0},{64,72},{72,64},{16,24},{24,16},{80,88},{88,80},{32,40... | collective-permute-start | bytes 1376264 | tf_op jit(solution)/shard_map/ppermute | solution.py:317
  53.3 25.2 %collective-permute-start.1 = (bf16[2,128,896]{2,1,0:T(8,128)(2,1)}, bf16[2,128,896]{2,1,0:T(8,128)(2,1)S(1)}, u32[]{:S(2)}, u32[]{:S(2)}) collective-permute-start(bf16[2,128,896]{2,1,0:T(8,128)(2,1)} %get-tuple-element.23), channel_id=1, source_target_pairs={{0,64},{8,72},{64,0},{72,8},{16,80},{24,88},{80,16},{88,24},{32,96... | collective-permute-start | bytes 1376264 | tf_op jit(solution)/shard_map/ppermute | solution.py:317
  56.4 22.1 %collective-permute-start.2 = (bf16[2,128,896]{2,1,0:T(8,128)(2,1)}, bf16[2,128,896]{2,1,0:T(8,128)(2,1)S(1)}, u32[]{:S(2)}, u32[]{:S(2)}) collective-permute-start(bf16[2,128,896]{2,1,0:T(8,128)(2,1)} %get-tuple-element.24), channel_id=1, source_target_pairs={{0,72},{8,64},{64,8},{72,0},{16,88},{24,80},{80,24},{88,16},{32,10... | collective-permute-start | bytes 1376264 | tf_op jit(solution)/shard_map/ppermute | solution.py:317
  61.7 1.0 copy-start.9
  61.8 1.1 copy-start.8
  63.0 14.8 %copy-start.6 = (bf16[128,128]{1,0:T(8,128)(2,1)S(1)}, bf16[128,128]{1,0:T(8,128)(2,1)}, u32[]{:S(2)}) copy-start(bf16[128,128]{1,0:T(8,128)(2,1)} %residual_ref.1) | copy-start | bytes 98308
  77.7 0.7 copy-start.7

commit v2 on v1

--- a/solution.py
+++ b/solution.py
@@ -241,7 +241,7 @@
             term = jnp.dot(hidden, weights[k][i], preferred_element_type=jnp.float32)
             totals[i] = term if totals[i] is None else totals[i] + term
     gate, up = [total.T for total in totals]
-    extra = padded(parts_of(squares, 2), STATS)
+    extra = padded(parts_of(squares, 2), EXTRA)
     for q in range(BLOCKS):
         part = slice(units * q, units * (q + 1))
         out_ref[q] = jnp.concatenate([gate[part], up[part], extra], axis=0).astype(jnp.bfloat16)
@@ -325,19 +325,21 @@
         scratch=[pltpu.VMEM((rows, HD), jnp.float32)],
     )
     gathered = exchange(own, None)
-    attention = (
-        gathered.reshape(bands, heads, band, HD).transpose(0, 2, 1, 3).reshape(branches, heads * HD)
-    )
-
-    projected = jnp.dot(attention, out_weight, preferred_element_type=jnp.float32)
+    gathered, *both = lax.optimization_barrier((gathered, *both))
+    by_branch = lambda a: (
+        a.reshape(bands, heads, band, HD).transpose(0, 2, 1, 3).reshape(branches, heads * HD)
+    )
+
+    projected = jnp.dot(by_branch(gathered), out_weight, preferred_element_type=jnp.float32)
     hidden, message = call(
         combine, (bf16(branches, width), bf16(QUAD, branches + EXTRA, width)), "combine",
         gather(projected.astype(jnp.bfloat16), "kvh", n_kvh), residual, norm_gain.reshape(1, width),
     )
-    message, *both = lax.optimization_barrier((message, *both))
+    hiddens, gathered = lax.optimization_barrier((exchange(message, P_GROUPS), gathered))
+    attention = by_branch(gathered)
     message = call(
-        functools.partial(gate_up, units), bf16(BLOCKS, 2 * units + STATS, branches), "gate_up",
-        exchange(message, P_GROUPS), *both,
+        functools.partial(gate_up, units), bf16(BLOCKS, 2 * units + EXTRA, branches), "gate_up",
+        hiddens, *both,
     )
     activation = call(
         functools.partial(activate, units), bf16(pad, branches), "activate",

time: 161 us -> 176 us (1.093)
  waiting for transfers between devices: 2.89 us -> 25.7 us
  blocking collectives: 127 us -> 111 us
  starting transfers between devices: 14.4 us -> 21.7 us
    ppermute x3, waiting for transfers between devices: 0.01 us -> 20 us  [on_device(): lax.ppermute(x, 'seq', [(seq_at(p, q), seq_at(p ^ k, q)) for q in range(B...]
    all_to_all x3 -> x2, blocking collectives: 62.7 us -> 44.7 us  [gather(): lax.all_to_all(copies, axis, 0, 0, axis_index_groups=groups, tiled=True)]
    all_to_all x0 -> x1, starting transfers between devices: none -> 7.32 us  [gather(): lax.all_to_all(copies, axis, 0, 0, axis_index_groups=groups, tiled=True)]
    all_to_all x0 -> x1, waiting for transfers between devices: none -> 5.7 us  [gather(): lax.all_to_all(copies, axis, 0, 0, axis_index_groups=groups, tiled=True)]
    all_to_all x1, waiting for transfers between devices: 2.88 us -> 0.01 us  [exchange(): return lax.all_to_all(x, 'seq', 0, 0, axis_index_groups=groups, tiled=True)]
    all_to_all x3, blocking collectives: 64.3 us -> 66.3 us  [exchange(): return lax.all_to_all(x, 'seq', 0, 0, axis_index_groups=groups, tiled=True)]
  transfers between devices with their start and end apart: 4 -> 5, of which waited for: 1 -> 3; matrix products, arithmetic and copies ran while one was open for 0% -> 0% of each run, Pallas kernels for 1% -> 0%
where the time goes in v2:
time: 176 us; the launch traced here: 175 us
  blocking collectives  111 us (63%)
  waiting for transfers between devices  25.7 us (15%)
  starting transfers between devices  21.7 us (12%)
  Pallas kernels  11.2 us (6%)
  local copies, waits for them, and re-layouts  3.35 us (2%)
    all_to_all x3, blocking collectives, exchange(): return lax.all_to_all(x, 'seq', 0, 0, axis_index_groups=groups, tiled=True)  66.3 us
    all_to_all x2, blocking collectives, gather(): lax.all_to_all(copies, axis, 0, 0, axis_index_groups=groups, tiled=True)  44.7 us
    ppermute x3, waiting for transfers between devices, on_device(): lax.ppermute(x, 'seq', [(seq_at(p, q), seq_at(p ^ k, q)) for q in range(B...  20 us
    pallas_call x6, Pallas kernels, call(): pl.pallas_call(kernel, out_shape=outs, in_specs=[spec(i) for i in range(l...  11.2 us
    ppermute x3, starting transfers between devices, on_device(): lax.ppermute(x, 'seq', [(seq_at(p, q), seq_at(p ^ k, q)) for q in range(B...  8.37 us
    all_to_all x1, starting transfers between devices, gather(): lax.all_to_all(copies, axis, 0, 0, axis_index_groups=groups, tiled=True)  7.32 us
    all_to_all x1, starting transfers between devices, exchange(): return lax.all_to_all(x, 'seq', 0, 0, axis_index_groups=groups, tiled=True)  6 us
    all_to_all x1, waiting for transfers between devices, gather(): lax.all_to_all(copies, axis, 0, 0, axis_index_groups=groups, tiled=True)  5.7 us
  transfers between devices with their start and end apart: 5, of which 3 were waited for; matrix products, arithmetic and copies ran while one was open for 0% of the time, Pallas kernels for 0%

profile of v2, /device:TPU:1, one launch (start us, length us, event | category | flops | bytes accessed | tf_op | source)
XLA Modules:
  0.0 175.1 jit_solution(2578243536405492868)
XLA Ops:
  0.7 8.7 %attend.1 = bf16[64,24,128]{2,1,0:T(8,128)(2,1)} custom-call(s32[1,128]{1,0:T(1,128)} %bitcast.29, s32[1,128]{1,0:T(1,128)} %bitcast.30, bf16[128,1024]{1,0:T(8,128)(2,1)} %q_ref.1, bf16[2048,128]{1,0:T(8,128)(2,1)} %k_hbm.1, bf16[2048,128]{1,0:T(8,128)(2,1)} %v_hbm.1, bf16[128,16,128]{2,1,0:T(8,128)(2,1)} %sk_hbm.1, bf16[128,16,128]{2,1,0:T(8,128)(2,1)} %sv_hbm.1), custom_call_target="tpu_custom_call" | custom-call | tf_op jit(solution)/shard_map/attend/pallas_call | solution.py:262
  9.4 32.3 %all_to_all.35.got_ref = bf16[64,24,128]{2,1,0:T(8,128)(2,1)S(1)} all-to-all(bf16[64,24,128]{2,1,0:T(8,128)(2,1)} %attend.1), channel_id=1, replica_groups=mesh['seq'=64,'kvh'=8] {'seq'}, dimensions={0} | all-to-all | bytes 786432 | tf_op jit(solution)/shard_map/all_to_all | solution.py:273
  41.8 1.4 finish.1
  43.1 6.0 %all-to-all-start.1 = ((bf16[64,16,128]{2,1,0:T(8,128)(2,1)}), bf16[64,16,128]{2,1,0:T(8,128)(2,1)S(1)}, u32[]{:S(2)}, u32[]{:S(2)}) async-start(bf16[64,16,128]{2,1,0:T(8,128)(2,1)} %finish.1), calls=%async_computation.1 | async-start | bytes 524288 | tf_op jit(solution)/shard_map/all_to_all | solution.py:273
  49.2 0.2 arrange.1
  49.3 2.9 %collective-permute-start = (bf16[2,128,896]{2,1,0:T(8,128)(2,1)S(1)}, bf16[2,128,896]{2,1,0:T(8,128)(2,1)S(1)}, u32[]{:S(2)}, u32[]{:S(2)}) collective-permute-start(bf16[2,128,896]{2,1,0:T(8,128)(2,1)S(1)} %get-tuple-element.22), channel_id=1, source_target_pairs={{0,8},{8,0},{64,72},{72,64},{16,24},{24,16},{80,88},{88,80},{32,40... | collective-permute-start | bytes 1376264 | tf_op jit(solution)/shard_map/ppermute | solution.py:317
  52.3 3.1 %collective-permute-start.1 = (bf16[2,128,896]{2,1,0:T(8,128)(2,1)S(1)}, bf16[2,128,896]{2,1,0:T(8,128)(2,1)S(1)}, u32[]{:S(2)}, u32[]{:S(2)}) collective-permute-start(bf16[2,128,896]{2,1,0:T(8,128)(2,1)S(1)} %get-tuple-element.23), channel_id=1, source_target_pairs={{0,64},{8,72},{64,0},{72,8},{16,80},{24,88},{80,16},{88,24},{32,96... | collective-permute-start | bytes 1376264 | tf_op jit(solution)/shard_map/ppermute | solution.py:317
  55.4 2.4 %collective-permute-start.2 = (bf16[2,128,896]{2,1,0:T(8,128)(2,1)S(1)}, bf16[2,128,896]{2,1,0:T(8,128)(2,1)S(1)}, u32[]{:S(2)}, u32[]{:S(2)}) collective-permute-start(bf16[2,128,896]{2,1,0:T(8,128)(2,1)S(1)} %get-tuple-element.24), channel_id=1, source_target_pairs={{0,72},{8,64},{64,8},{72,0},{16,88},{24,80},{80,24},{88,16},{32,10... | collective-permute-start | bytes 1376264 | tf_op jit(solution)/shard_map/ppermute | solution.py:317
  57.7 7.7 %collective-permute-done.refs_1_ = bf16[2,128,896]{2,1,0:T(8,128)(2,1)S(1)} collective-permute-done((bf16[2,128,896]{2,1,0:T(8,128)(2,1)S(1)}, bf16[2,128,896]{2,1,0:T(8,128)(2,1)S(1)}, u32[]{:S(2)}, u32[]{:S(2)}) %collective-permute-start) | collective-permute-done | bytes 458784 | tf_op jit(solution)/shard_map/ppermute | solution.py:317
  65.4 12.3 %collective-permute-done.1.refs_2_ = bf16[2,128,896]{2,1,0:T(8,128)(2,1)S(1)} collective-permute-done((bf16[2,128,896]{2,1,0:T(8,128)(2,1)S(1)}, bf16[2,128,896]{2,1,0:T(8,128)(2,1)S(1)}, u32[]{:S(2)}, u32[]{:S(2)}) %collective-permute-start.1) | collective-permute-done | bytes 458784 | tf_op jit(solution)/shard_map/ppermute | solution.py:317
  77.9 0.9 copy-done.8
  78.7 0.2 convolution_convert_fusion.1
  79.0 12.2 %all_to_all.36.got_ref = bf16[8,128,128]{2,1,0:T(8,128)(2,1)S(1)} all-to-all(bf16[8,128,128]{2,1,0:T(8,128)(2,1)S(1)} %broadcast_in_dim.9), channel_id=1, replica_groups=mesh['seq'=64,'kvh'=8] {'kvh'}, dimensions={0} | all-to-all | bytes 524288 | tf_op jit(solution)/shard_map/all_to_all | solution.py:278
  91.2 0.7 copy-done.7
  92.0 7.0 %all_to_all.37.hidden_ref = bf16[4,144,128]{2,1,0:T(8,128)(2,1)S(1)} all-to-all(bf16[4,144,128]{2,1,0:T(8,128)(2,1)S(1)} %get-tuple-element.26), channel_id=1, replica_groups={{0,8,64,72},{16,24,80,88},{32,40,96,104},{48,56,112,120},{128,136,192,2..., dimensions={0} | all-to-all | bytes 294912 | tf_op jit(solution)/shard_map/all_to_all | solution.py:273
  99.1 0.7 gate_up.1
  99.8 26.9 %all_to_all.38.got_ref = bf16[16,128,128]{2,1,0:T(8,128)(2,1)S(1)} all-to-all(bf16[16,128,128]{2,1,0:T(8,128)(2,1)S(1)} %gate_up.1), channel_id=1, replica_groups={{0,16,32,48,128,144,160,176,256,272,288,304,384,400,416,432},{8,24,40,5..., dimensions={0} | all-to-all | bytes 1048576 | tf_op jit(solution)/shard_map/all_to_all | solution.py:273
  126.9 32.5 %all_to_all.39 = bf16[64,56,128]{2,1,0:T(8,128)(2,1)S(1)} all-to-all(bf16[64,56,128]{2,1,0:T(8,128)(2,1)S(1)} %broadcast_in_dim.10), channel_id=1, replica_groups={{0,16,32,48,128,144,160,176,256,272,288,304,384,400,416,432,8,24,40,56,..., dimensions={0} | all-to-all | bytes 1835008 | tf_op jit(solution)/shard_map/all_to_all | solution.py:278
  159.4 0.4 convolution_convert_fusion
  159.9 0.7 broadcast_in_dim.11
  160.6 7.3 %all-to-all-start.6 = ((bf16[8,128,128]{2,1,0:T(8,128)(2,1)}), bf16[8,128,128]{2,1,0:T(8,128)(2,1)S(1)}, u32[]{:S(2)}, u32[]{:S(2)}) async-start(bf16[8,128,128]{2,1,0:T(8,128)(2,1)} %broadcast_in_dim.11), calls=%async_computation.6 | async-start | bytes 524288 | tf_op jit(solution)/shard_map/all_to_all | solution.py:278
  168.0 0.8 copy.29
  168.7 5.7 %all-to-all-done.6 = bf16[8,128,128]{2,1,0:T(8,128)(2,1)S(1)} async-done(((bf16[8,128,128]{2,1,0:T(8,128)(2,1)}), bf16[8,128,128]{2,1,0:T(8,128)(2,1)S(1)}, u32[]{:S(2)}, u32[]{:S(2)}) %all-to-all-start.6) | async-done | bytes 262176 | tf_op jit(solution)/shard_map/all_to_all | solution.py:278
  174.5 0.6 add_convert_fusion
  (26 shorter events, 0.6 us)
Async XLA Ops:
  0.6 158.8 %copy-start = (bf16[3584,128]{1,0:T(8,128)(2,1)S(1)}, bf16[3584,128]{1,0:T(8,128)(2,1)}, u32[]{:S(2)}) copy-start(bf16[3584,128]{1,0:T(8,128)(2,1)} %param.29) | copy-start | bytes 2752516
  0.6 41.1 %copy-start.4 = (bf16[128,128]{1,0:T(8,128)(2,1)S(1)}, bf16[128,128]{1,0:T(8,128)(2,1)}, u32[]{:S(2)}) copy-start(bf16[128,128]{1,0:T(8,128)(2,1)} %nk_ref.1) | copy-start | bytes 98308
  0.7 41.1 %copy-start.5 = (bf16[128,128]{1,0:T(8,128)(2,1)S(1)}, bf16[128,128]{1,0:T(8,128)(2,1)}, u32[]{:S(2)}) copy-start(bf16[128,128]{1,0:T(8,128)(2,1)} %nv_ref.1) | copy-start | bytes 98308
  9.4 32.4 %copy-start.1 = (bf16[128,1024]{1,0:T(8,128)(2,1)S(1)}, bf16[128,1024]{1,0:T(8,128)(2,1)}, u32[]{:S(2)}) copy-start(bf16[128,1024]{1,0:T(8,128)(2,1)} %q_ref.1) | copy-start | bytes 786436
  9.4 39.7 %copy-start.3 = (bf16[128,3584]{1,0:T(8,128)(2,1)S(1)}, bf16[128,3584]{1,0:T(8,128)(2,1)}, u32[]{:S(2)}) copy-start(bf16[128,3584]{1,0:T(8,128)(2,1)} %up_ref) | copy-start | bytes 2752516
  41.8 7.4 %copy-start.2 = (bf16[128,3584]{1,0:T(8,128)(2,1)S(1)}, bf16[128,3584]{1,0:T(8,128)(2,1)}, u32[]{:S(2)}) copy-start(bf16[128,3584]{1,0:T(8,128)(2,1)} %gate_ref) | copy-start | bytes 2752516
  43.1 34.6 %all-to-all-start.1 = ((bf16[64,16,128]{2,1,0:T(8,128)(2,1)}), bf16[64,16,128]{2,1,0:T(8,128)(2,1)S(1)}, u32[]{:S(2)}, u32[]{:S(2)}) async-start(bf16[64,16,128]{2,1,0:T(8,128)(2,1)} %finish.1), calls=%async_computation.1 | async-start | bytes 524288 | tf_op jit(solution)/shard_map/all_to_all | solution.py:273
  49.3 16.1 %collective-permute-start = (bf16[2,128,896]{2,1,0:T(8,128)(2,1)S(1)}, bf16[2,128,896]{2,1,0:T(8,128)(2,1)S(1)}, u32[]{:S(2)}, u32[]{:S(2)}) collective-permute-start(bf16[2,128,896]{2,1,0:T(8,128)(2,1)S(1)} %get-tuple-element.22), channel_id=1, source_target_pairs={{0,8},{8,0},{64,72},{72,64},{16,24},{24,16},{80,88},{88,80},{32,40... | collective-permute-start | bytes 1376264 | tf_op jit(solution)/shard_map/ppermute | solution.py:317
  52.3 25.5 %collective-permute-start.1 = (bf16[2,128,896]{2,1,0:T(8,128)(2,1)S(1)}, bf16[2,128,896]{2,1,0:T(8,128)(2,1)S(1)}, u32[]{:S(2)}, u32[]{:S(2)}) collective-permute-start(bf16[2,128,896]{2,1,0:T(8,128)(2,1)S(1)} %get-tuple-element.23), channel_id=1, source_target_pairs={{0,64},{8,72},{64,0},{72,8},{16,80},{24,88},{80,16},{88,24},{32,96... | collective-permute-start | bytes 1376264 | tf_op jit(solution)/shard_map/ppermute | solution.py:317
  55.4 22.4 %collective-permute-start.2 = (bf16[2,128,896]{2,1,0:T(8,128)(2,1)S(1)}, bf16[2,128,896]{2,1,0:T(8,128)(2,1)S(1)}, u32[]{:S(2)}, u32[]{:S(2)}) collective-permute-start(bf16[2,128,896]{2,1,0:T(8,128)(2,1)S(1)} %get-tuple-element.24), channel_id=1, source_target_pairs={{0,72},{8,64},{64,8},{72,0},{16,88},{24,80},{80,24},{88,16},{32,10... | collective-permute-start | bytes 1376264 | tf_op jit(solution)/shard_map/ppermute | solution.py:317
  77.8 1.0 copy-start.8
  79.0 12.2 %copy-start.6 = (bf16[128,128]{1,0:T(8,128)(2,1)S(1)}, bf16[128,128]{1,0:T(8,128)(2,1)}, u32[]{:S(2)}) copy-start(bf16[128,128]{1,0:T(8,128)(2,1)} %residual_ref.1) | copy-start | bytes 98308
  91.2 0.7 copy-start.7
  160.6 13.8 %all-to-all-start.6 = ((bf16[8,128,128]{2,1,0:T(8,128)(2,1)}), bf16[8,128,128]{2,1,0:T(8,128)(2,1)S(1)}, u32[]{:S(2)}, u32[]{:S(2)}) async-start(bf16[8,128,128]{2,1,0:T(8,128)(2,1)} %broadcast_in_dim.11), calls=%async_computation.6 | async-start | bytes 524288 | tf_op jit(solution)/shard_map/all_to_all | solution.py:278

commit v3 on v0

--- a/solution.py
+++ b/solution.py
@@ -103,7 +103,7 @@
 
 def attend(bands, band, heads, offsets_ref, lengths_ref, q_hbm, k_hbm, v_hbm, sk_hbm, sv_hbm, out_ref,
            q_ref, k_ref, v_ref, sk_ref, sv_ref, vt_ref, off_ref, len_ref, tail_pos_ref,
-           sems):
+           weight_ref, tail_weight_ref, peak_ref, sems):
     context = k_ref.shape[0]
     tail = sk_ref.shape[1]
     cols = heads * band
@@ -121,7 +121,7 @@
     def queries_of(g):
         return head_rows(q_ref[pl.ds(pl.multiple_of(g * band, band), band), :], heads)
 
-    def pair(p, first):
+    def weigh(p, first):
         bases = (2 * p, 2 * p + 1)
         if first:
             waits[0]()
@@ -145,27 +145,33 @@
             tails.append(jnp.where(tail_pos_ref[...] < length, tail_scores, NEG_FILL))
         tail_peak = jnp.concatenate([jnp.max(t, axis=0, keepdims=True) for t in tails], axis=1)
         peak = jnp.maximum(peak, tail_peak)
-        weights = jnp.exp2((scores - peak) * SCALE_LOG2).astype(jnp.bfloat16)
-        if first:
-            waits[3]()
-            vt_ref[...] = with_ones(v_ref[...])
-            waits[4]()
-        sums = jnp.dot(vt_ref[...], weights, preferred_element_type=jnp.float32)
+        weight_ref[p] = jnp.exp2((scores - peak) * SCALE_LOG2).astype(jnp.bfloat16)
         for i, g in enumerate(bases):
+            own_peak = peak[:, i * cols : (i + 1) * cols]
+            peak_ref[pl.ds(g, 1), :] = own_peak
+            tail_weight_ref[g] = jnp.exp2((tails[i] - own_peak) * SCALE_LOG2).astype(jnp.bfloat16)
+
+    def add_up(p):
+        sums = jnp.dot(vt_ref[...], weight_ref[p], preferred_element_type=jnp.float32)
+        for i, g in enumerate((2 * p, 2 * p + 1)):
             at = pl.multiple_of(g * band, band)
-            own = slice(i * cols, (i + 1) * cols)
-            own_peak = peak[:, own]
-            tail_weights = jnp.exp2((tails[i] - own_peak) * SCALE_LOG2).astype(jnp.bfloat16)
             values = with_ones(sv_ref[pl.ds(at, band)].reshape(band * tail, HD))
-            full = sums[:, own] + jnp.dot(values, tail_weights, preferred_element_type=jnp.float32)
+            full = sums[:, i * cols : (i + 1) * cols] + jnp.dot(
+                values, tail_weight_ref[g], preferred_element_type=jnp.float32
+            )
+            own_peak = peak_ref[pl.ds(g, 1), :]
             some = own_peak > 0.5 * NEG_FILL
             total = jnp.where(some, full[HD : HD + 1], 0.0)
             output = jnp.where(some, full[:HD], 0.0).T
             stats = padded(parts_of(own_peak, 3) + parts_of(total, 2), EXTRA)
             out_ref[g] = jnp.concatenate([output, stats], axis=0).astype(jnp.bfloat16)
 
-    pair(0, True)
-    pl.loop(1, bands // 2)(lambda p: pair(p, False))
+    weigh(0, True)
+    pl.loop(1, bands // 2)(lambda p: weigh(p, False))
+    waits[3]()
+    vt_ref[...] = with_ones(v_ref[...])
+    waits[4]()
+    pl.loop(0, bands // 2)(add_up)
 
 
 def merged(got_ref):
@@ -288,6 +294,7 @@
     bands = SIDE
     band = branches // bands
     rows = heads * band
+    tail_rows = band * suffix_keys.shape[1]
     hidden_units = w_gate.shape[1]
     units = hidden_units // SIDE**2
     pad = -(-units // 16) * 16
@@ -306,7 +313,10 @@
                  like(suffix_values),
                  pltpu.VMEM((HD + EXTRA, prefix_keys.shape[0]), jnp.bfloat16),
                  pltpu.VMEM((bands, rows), jnp.int32), pltpu.VMEM((bands, rows), jnp.int32),
-                 pltpu.VMEM((band * suffix_keys.shape[1], rows), jnp.int32),
+                 pltpu.VMEM((tail_rows, rows), jnp.int32),
+                 pltpu.VMEM((bands // 2, prefix_keys.shape[0], 2 * rows), jnp.bfloat16),
+                 pltpu.VMEM((bands, tail_rows, rows), jnp.bfloat16),
+                 pltpu.VMEM((bands, rows), jnp.float32),
                  copies_sem(5)],
     )
     message, *moved = lax.optimization_barrier((message, w_gate, w_up))

time: 158 us -> 157 us (level)
  no operation moved by 1% of the time
where the time goes in v3:
time: 157 us; the launch traced here: 156 us
  blocking collectives  127 us (81%)
  Pallas kernels  12.5 us (8%)
  starting transfers between devices  12.4 us (8%)
  local copies, waits for them, and re-layouts  1.9 us (1%)
    all_to_all x4, blocking collectives, exchange(): return lax.all_to_all(x, 'seq', 0, 0, axis_index_groups=groups, tiled=True)  66.9 us
    all_to_all x3, blocking collectives, gather(): lax.all_to_all(copies, axis, 0, 0, axis_index_groups=groups, tiled=True)  59.8 us
    pallas_call x7, Pallas kernels, call(): pl.pallas_call(kernel, out_shape=outs, in_specs=[spec(i) for i in range(l...  12.5 us
    ppermute x3, starting transfers between devices, on_device(): lax.ppermute(x, 'seq', [(seq_at(p, q), seq_at(p ^ k, q)) for q in range(B...  8.36 us
    all_to_all x1, starting transfers between devices, exchange(): return lax.all_to_all(x, 'seq', 0, 0, axis_index_groups=groups, tiled=True)  4.03 us
  transfers between devices with their start and end apart: 4, of which 0 were waited for; matrix products, arithmetic and copies ran while one was open for 0% of the time, Pallas kernels for 1%

profile of v3, /device:TPU:1, one launch (start us, length us, event | category | flops | bytes accessed | tf_op | source)
XLA Modules:
  0.0 155.8 jit_solution(15639975844425556817)
XLA Ops:
  0.6 8.7 %attend.1 = bf16[8,144,128]{2,1,0:T(8,128)(2,1)} custom-call(s32[1,128]{1,0:T(1,128)} %bitcast.22, s32[1,128]{1,0:T(1,128)} %bitcast.23, bf16[128,1024]{1,0:T(8,128)(2,1)} %q_ref.1, bf16[2048,128]{1,0:T(8,128)(2,1)} %k_hbm.1, bf16[2048,128]{1,0:T(8,128)(2,1)} %v_hbm.1, bf16[128,16,128]{2,1,0:T(8,128)(2,1)} %sk_hbm.1, bf16[128,16,128]{2,1,0:T(8,128)(2,1)} %sv_hbm.1), custom_call_target="tpu_custom_call" | custom-call | tf_op jit(solution)/shard_map/attend/pallas_call | solution.py:270
  9.4 21.7 %all_to_all.40.got_ref = bf16[8,144,128]{2,1,0:T(8,128)(2,1)S(1)} all-to-all(bf16[8,144,128]{2,1,0:T(8,128)(2,1)} %attend.1), channel_id=1, replica_groups={{0,64,128,192,256,320,384,448},{8,72,136,200,264,328,392,456},{16,80,14..., dimensions={0} | all-to-all | bytes 589824 | tf_op jit(solution)/shard_map/all_to_all | solution.py:281
  31.1 0.4 merge.1
  31.5 16.5 %all_to_all.41.got_ref = bf16[8,144,128]{2,1,0:T(8,128)(2,1)S(1)} all-to-all(bf16[8,144,128]{2,1,0:T(8,128)(2,1)S(1)} %merge.1), channel_id=1, replica_groups={{0,8,16,24,32,40,48,56},{64,72,80,88,96,104,112,120},{128,136,144,152,1..., dimensions={0} | all-to-all | bytes 589824 | tf_op jit(solution)/shard_map/all_to_all | solution.py:281
  47.9 1.3 finish.1
  49.3 4.0 %all-to-all-start.2 = ((bf16[8,128,128]{2,1,0:T(8,128)(2,1)}), bf16[8,128,128]{2,1,0:T(8,128)(2,1)S(1)}, u32[]{:S(2)}, u32[]{:S(2)}) async-start(bf16[8,128,128]{2,1,0:T(8,128)(2,1)} %finish.1), calls=%async_computation.2 | async-start | bytes 524288 | tf_op jit(solution)/shard_map/all_to_all | solution.py:281
  53.3 1.2 arrange.1
  54.5 1.9 %collective-permute-start = (bf16[2,128,896]{2,1,0:T(8,128)(2,1)}, bf16[2,128,896]{2,1,0:T(8,128)(2,1)S(1)}, u32[]{:S(2)}, u32[]{:S(2)}) collective-permute-start(bf16[2,128,896]{2,1,0:T(8,128)(2,1)} %get-tuple-element.22), channel_id=1, source_target_pairs={{0,8},{8,0},{64,72},{72,64},{16,24},{24,16},{80,88},{88,80},{32,40... | collective-permute-start | bytes 1376264 | tf_op jit(solution)/shard_map/ppermute | solution.py:325
  56.4 3.4 %collective-permute-start.1 = (bf16[2,128,896]{2,1,0:T(8,128)(2,1)}, bf16[2,128,896]{2,1,0:T(8,128)(2,1)S(1)}, u32[]{:S(2)}, u32[]{:S(2)}) collective-permute-start(bf16[2,128,896]{2,1,0:T(8,128)(2,1)} %get-tuple-element.23), channel_id=1, source_target_pairs={{0,64},{8,72},{64,0},{72,8},{16,80},{24,88},{80,16},{88,24},{32,96... | collective-permute-start | bytes 1376264 | tf_op jit(solution)/shard_map/ppermute | solution.py:325
  59.8 3.1 %collective-permute-start.2 = (bf16[2,128,896]{2,1,0:T(8,128)(2,1)}, bf16[2,128,896]{2,1,0:T(8,128)(2,1)S(1)}, u32[]{:S(2)}, u32[]{:S(2)}) collective-permute-start(bf16[2,128,896]{2,1,0:T(8,128)(2,1)} %get-tuple-element.24), channel_id=1, source_target_pairs={{0,72},{8,64},{64,8},{72,0},{16,88},{24,80},{80,24},{88,16},{32,10... | collective-permute-start | bytes 1376264 | tf_op jit(solution)/shard_map/ppermute | solution.py:325
  63.1 0.9 copy-done.9
  63.9 0.2 convolution_convert_fusion.1
  64.2 15.2 %all_to_all.42.got_ref = bf16[8,128,128]{2,1,0:T(8,128)(2,1)S(1)} all-to-all(bf16[8,128,128]{2,1,0:T(8,128)(2,1)S(1)} %broadcast_in_dim.9), channel_id=1, replica_groups=mesh['seq'=64,'kvh'=8] {'kvh'}, dimensions={0} | all-to-all | bytes 524288 | tf_op jit(solution)/shard_map/all_to_all | solution.py:286
  79.4 0.7 copy-done.7
  80.1 0.1 combine.1
  80.2 6.7 %all_to_all.43.hidden_ref = bf16[4,144,128]{2,1,0:T(8,128)(2,1)S(1)} all-to-all(bf16[4,144,128]{2,1,0:T(8,128)(2,1)S(1)} %get-tuple-element.25), channel_id=1, replica_groups={{0,8,64,72},{16,24,80,88},{32,40,96,104},{48,56,112,120},{128,136,192,2..., dimensions={0} | all-to-all | bytes 294912 | tf_op jit(solution)/shard_map/all_to_all | solution.py:281
  87.0 0.7 gate_up.1
  87.7 22.0 %all_to_all.44.got_ref = bf16[16,128,128]{2,1,0:T(8,128)(2,1)S(1)} all-to-all(bf16[16,128,128]{2,1,0:T(8,128)(2,1)S(1)} %gate_up.1), channel_id=1, replica_groups={{0,16,32,48,128,144,160,176,256,272,288,304,384,400,416,432},{8,24,40,5..., dimensions={0} | all-to-all | bytes 1048576 | tf_op jit(solution)/shard_map/all_to_all | solution.py:281
  109.7 0.1 activate.1
  109.8 0.1 broadcast_in_dim.10
  109.9 26.4 %all_to_all.45 = bf16[64,56,128]{2,1,0:T(8,128)(2,1)S(1)} all-to-all(bf16[64,56,128]{2,1,0:T(8,128)(2,1)S(1)} %broadcast_in_dim.10), channel_id=1, replica_groups={{0,16,32,48,128,144,160,176,256,272,288,304,384,400,416,432,8,24,40,56,..., dimensions={0} | all-to-all | bytes 1835008 | tf_op jit(solution)/shard_map/all_to_all | solution.py:286
  136.3 0.4 convolution_convert_fusion
  136.8 18.3 %all_to_all.46 = bf16[8,128,128]{2,1,0:T(8,128)(2,1)S(1)} all-to-all(bf16[8,128,128]{2,1,0:T(8,128)(2,1)S(1)} %broadcast_in_dim.11), channel_id=1, replica_groups=mesh['seq'=64,'kvh'=8] {'kvh'}, dimensions={0} | all-to-all | bytes 524288 | tf_op jit(solution)/shard_map/all_to_all | solution.py:286
  155.1 0.6 add_convert_fusion
  (28 shorter events, 0.3 us)
Async XLA Ops:
  0.6 135.7 %copy-start = (bf16[3584,128]{1,0:T(8,128)(2,1)S(1)}, bf16[3584,128]{1,0:T(8,128)(2,1)}, u32[]{:S(2)}) copy-start(bf16[3584,128]{1,0:T(8,128)(2,1)} %param.29) | copy-start | bytes 2752516
  9.3 38.6 %copy-start.4 = (bf16[128,128]{1,0:T(8,128)(2,1)S(1)}, bf16[128,128]{1,0:T(8,128)(2,1)}, u32[]{:S(2)}) copy-start(bf16[128,128]{1,0:T(8,128)(2,1)} %nk_ref.1) | copy-start | bytes 98308
  9.3 38.6 %copy-start.5 = (bf16[128,128]{1,0:T(8,128)(2,1)S(1)}, bf16[128,128]{1,0:T(8,128)(2,1)}, u32[]{:S(2)}) copy-start(bf16[128,128]{1,0:T(8,128)(2,1)} %nv_ref.1) | copy-start | bytes 98308
  31.1 22.2 %copy-start.3 = (bf16[128,3584]{1,0:T(8,128)(2,1)S(1)}, bf16[128,3584]{1,0:T(8,128)(2,1)}, u32[]{:S(2)}) copy-start(bf16[128,3584]{1,0:T(8,128)(2,1)} %up_ref) | copy-start | bytes 2752516
  31.5 16.5 %copy-start.1 = (bf16[128,1024]{1,0:T(8,128)(2,1)S(1)}, bf16[128,1024]{1,0:T(8,128)(2,1)}, u32[]{:S(2)}) copy-start(bf16[128,1024]{1,0:T(8,128)(2,1)} %q_ref.1) | copy-start | bytes 786436
  31.5 21.8 %copy-start.2 = (bf16[128,3584]{1,0:T(8,128)(2,1)S(1)}, bf16[128,3584]{1,0:T(8,128)(2,1)}, u32[]{:S(2)}) copy-start(bf16[128,3584]{1,0:T(8,128)(2,1)} %gate_ref) | copy-start | bytes 2752516
  49.3 13.6 %all-to-all-start.2 = ((bf16[8,128,128]{2,1,0:T(8,128)(2,1)}), bf16[8,128,128]{2,1,0:T(8,128)(2,1)S(1)}, u32[]{:S(2)}, u32[]{:S(2)}) async-start(bf16[8,128,128]{2,1,0:T(8,128)(2,1)} %finish.1), calls=%async_computation.2 | async-start | bytes 524288 | tf_op jit(solution)/shard_map/all_to_all | solution.py:281
  54.5 25.7 %collective-permute-start = (bf16[2,128,896]{2,1,0:T(8,128)(2,1)}, bf16[2,128,896]{2,1,0:T(8,128)(2,1)S(1)}, u32[]{:S(2)}, u32[]{:S(2)}) collective-permute-start(bf16[2,128,896]{2,1,0:T(8,128)(2,1)} %get-tuple-element.22), channel_id=1, source_target_pairs={{0,8},{8,0},{64,72},{72,64},{16,24},{24,16},{80,88},{88,80},{32,40... | collective-permute-start | bytes 1376264 | tf_op jit(solution)/shard_map/ppermute | solution.py:325
  56.4 23.8 %collective-permute-start.1 = (bf16[2,128,896]{2,1,0:T(8,128)(2,1)}, bf16[2,128,896]{2,1,0:T(8,128)(2,1)S(1)}, u32[]{:S(2)}, u32[]{:S(2)}) collective-permute-start(bf16[2,128,896]{2,1,0:T(8,128)(2,1)} %get-tuple-element.23), channel_id=1, source_target_pairs={{0,64},{8,72},{64,0},{72,8},{16,80},{24,88},{80,16},{88,24},{32,96... | collective-permute-start | bytes 1376264 | tf_op jit(solution)/shard_map/ppermute | solution.py:325
  59.8 20.4 %collective-permute-start.2 = (bf16[2,128,896]{2,1,0:T(8,128)(2,1)}, bf16[2,128,896]{2,1,0:T(8,128)(2,1)S(1)}, u32[]{:S(2)}, u32[]{:S(2)}) collective-permute-start(bf16[2,128,896]{2,1,0:T(8,128)(2,1)} %get-tuple-element.24), channel_id=1, source_target_pairs={{0,72},{8,64},{64,8},{72,0},{16,88},{24,80},{80,24},{88,16},{32,10... | collective-permute-start | bytes 1376264 | tf_op jit(solution)/shard_map/ppermute | solution.py:325
  63.0 1.0 copy-start.9
  63.1 1.1 copy-start.8
  64.2 15.2 %copy-start.6 = (bf16[128,128]{1,0:T(8,128)(2,1)S(1)}, bf16[128,128]{1,0:T(8,128)(2,1)}, u32[]{:S(2)}) copy-start(bf16[128,128]{1,0:T(8,128)(2,1)} %residual_ref.1) | copy-start | bytes 98308
  79.4 0.7 copy-start.7
